TPU v7x, 32 devices: a whole 2x2x4 slice. The times are simulated.
32 devices in a mesh: cfg: 2 (over core), seq: 4 (over z), blk: 4 (over y, x).
Axes of the slice: x: 2, y: 2, z: 4, core: 2. Of those that a mesh axis runs over, the one named last changes fastest.
Arguments:
- img_hidden: bfloat16 [2, 2, 2048, 1536], P('cfg', None, 'seq', 'blk'), may hold values from -15 to 15
- txt_hidden: bfloat16 [2, 2, 160, 1536], P('cfg', None, 'seq', 'blk'), may hold values from -6 to 6
- img_mod: float32 [2, 2, 6, 1536], P('cfg'), may hold values from -9 to 9
- txt_mod: float32 [2, 2, 2, 1536], P('cfg'), may hold values from -3 to 3
- out_mod: float32 [2, 2, 2, 1536], P('cfg'), may hold values from -3 to 3
- w_qkv: bfloat16 [3, 1536, 1536], P(None, None, 'blk'), may hold values from -0.25 to 0.25
- w_txt_kv: bfloat16 [2, 1536, 1536], P(None, None, 'blk'), may hold values from -0.25 to 0.25
- w_out: bfloat16 [1536, 1536], P('blk'), may hold values from -0.15625 to 0.15625
- w_fc1: bfloat16 [1536, 6144], P(None, 'blk'), may hold values from -0.15625 to 0.15625
- w_fc2: bfloat16 [6144, 1536], P('blk'), may hold values from -0.078125 to 0.078125
- w_proj: bfloat16 [1536, 64], P('blk'), may hold values from -0.15625 to 0.15625
- latent: float32 [2, 2048, 64], P(None, 'seq', 'cfg'), may hold values from -6 to 6
- lengths: int32 [2, 2], P('cfg'), may hold values from 1 to 154, as said below
- t_index: int32 [2], replicated, may hold values from 0 to 24
- stride: int32 [2], replicated, may hold values from 1 to 4
- guide: float32 [2], replicated, may hold values from 4 to 8
Outputs:
- new_latent: float32 [2, 2048, 64], P(None, 'seq', 'cfg')
- update_max: float32 [2], replicated
Inputs may be any that keep to these rules, and one draw needn't show every extreme that they name: `lengths`: at least one entry equals 154.
All inputs are finite; a program needn't handle non-finite values.
Results may differ from a plain program's by a relative error of at most 0.015.
Values may be sent and summed in bfloat16 or wider, within the bound.
A program may use at most 192 MiB of HBM per device.

v0:
```python
import jax
import jax.numpy as jnp
from jax import lax
from jax.sharding import PartitionSpec as P

HEAD = 64
STEPS = 28
EPSILON = 1e-06
BLOCK_ROWS = 512


def from_partner(value, axis, bit):
    return lax.ppermute(value, axis, [(i, i ^ 1 << bit) for i in range(lax.axis_size(axis))])


def normalize(values):
    values = values.astype(jnp.float32)
    center = jnp.mean(values, axis=-1, keepdims=True)
    spread = jnp.mean(jnp.square(values - center), axis=-1, keepdims=True)
    return (values - center) * lax.rsqrt(spread + EPSILON)


def modulate(values, scale_row, shift_row):
    return (normalize(values) * (1.0 + scale_row[:, None, :]) + shift_row[:, None, :]).astype(
        jnp.bfloat16
    )


def project(values, weight):
    flat_rows = values.reshape(-1, values.shape[-1])
    result = jnp.dot(flat_rows, weight, preferred_element_type=jnp.float32)
    return result.reshape(values.shape[:-1] + (weight.shape[-1],))


def noise_level(step_index):
    remain = 1.0 - step_index.astype(jnp.float32) / STEPS
    return 3.0 * remain / (1.0 + 2.0 * remain)


def own_columns(values, column_block, shard_width):
    return lax.dynamic_slice_in_dim(
        values, column_block * shard_width, shard_width, values.ndim - 1
    )


def per_device(
    img_hidden,
    txt_hidden,
    img_mod,
    txt_mod,
    out_mod,
    w_qkv,
    w_txt_kv,
    w_out,
    w_fc1,
    w_fc2,
    w_proj,
    latent,
    lengths,
    t_index,
    stride,
    guide,
):
    column_block = lax.axis_index("blk")
    shard_width = img_hidden.shape[3]
    model_width = shard_width * lax.axis_size("blk")
    image_full, text_full = (
        lax.all_gather(img_hidden[0], "blk", axis=2, tiled=True),
        lax.all_gather(txt_hidden[0], "blk", axis=2, tiled=True),
    )
    image_mod = img_mod[0]
    prompts = image_full.shape[0]
    img_rows = image_full.shape[1]
    attn_in = modulate(image_full, image_mod[:, 1], image_mod[:, 0])
    queries = project(attn_in, w_qkv[0]).astype(jnp.bfloat16)
    keys_img = project(attn_in, w_qkv[1]).astype(jnp.bfloat16)
    values_img = project(attn_in, w_qkv[2]).astype(jnp.bfloat16)
    text_norm = modulate(text_full, txt_mod[0][:, 0], txt_mod[0][:, 1])
    text_keys = project(text_norm, w_txt_kv[0]).astype(jnp.bfloat16)
    text_values = project(text_norm, w_txt_kv[1]).astype(jnp.bfloat16)
    head_width = queries.shape[2]
    head_count = head_width // HEAD
    query_heads = queries.reshape(prompts, img_rows, head_count, HEAD)
    text_limit = lengths[0]

    def attend_block(running_state, key_block, value_block, live_mask):
        accumulated, running, denominator = running_state
        key_count = key_block.shape[1]
        key_heads = key_block.reshape(prompts, key_count, head_count, HEAD)
        value_heads = value_block.reshape(prompts, key_count, head_count, HEAD)
        scores = jnp.einsum(
            "pqhe,pkhe->phqk", query_heads, key_heads, preferred_element_type=jnp.float32
        ) * HEAD ** (-0.5)
        if live_mask is not None:
            scores = jnp.where(live_mask[:, None, None, :], scores, -jnp.inf)
        updated = jnp.maximum(running, jnp.max(scores, axis=-1))
        factor = jnp.exp(running - updated)
        weights = jnp.exp(scores - updated[..., None])
        denominator = denominator * factor + jnp.sum(weights, axis=-1)
        mixed_values = jnp.einsum(
            "phqk,pkhe->phqe",
            weights.astype(jnp.bfloat16),
            value_heads,
            preferred_element_type=jnp.float32,
        )
        accumulated = accumulated * factor[..., None] + mixed_values
        return (accumulated, updated, denominator)

    initial = (
        jnp.zeros((prompts, head_count, img_rows, HEAD), jnp.float32),
        jnp.full((prompts, head_count, img_rows), -1e30, jnp.float32),
        jnp.zeros((prompts, head_count, img_rows), jnp.float32),
    )
    running_state = initial
    key_piece = lax.all_gather(keys_img, "seq", axis=1, tiled=True)
    value_piece = lax.all_gather(values_img, "seq", axis=1, tiled=True)
    key_count = key_piece.shape[1]
    blocks = key_count // BLOCK_ROWS
    key_split = key_piece.reshape(prompts, blocks, BLOCK_ROWS, head_width).transpose(1, 0, 2, 3)
    value_split = value_piece.reshape(prompts, blocks, BLOCK_ROWS, head_width).transpose(1, 0, 2, 3)

    def scan_step(state_now, operands):
        key_block, value_block = operands
        return (attend_block(state_now, key_block, value_block, None), None)

    running_state, unused = lax.scan(scan_step, running_state, (key_split, value_split))
    all_text_keys, all_text_values = (
        lax.all_gather(text_keys, "seq", axis=1, tiled=True),
        lax.all_gather(text_values, "seq", axis=1, tiled=True),
    )
    slot_index = jnp.arange(all_text_keys.shape[1], dtype=jnp.int32)
    text_mask = slot_index[None, :] < text_limit[:, None]
    accumulated, running, denominator = attend_block(
        running_state, all_text_keys, all_text_values, text_mask
    )
    attended = (accumulated / denominator[..., None]).astype(jnp.bfloat16)
    attended = attended.transpose(0, 2, 1, 3).reshape(prompts, img_rows, head_width)
    attn_part = project(attended, w_out)
    attn_sum = lax.psum(attn_part.astype(jnp.bfloat16), "blk").astype(jnp.float32)
    resid_full = (image_full.astype(jnp.float32) + image_mod[:, 2][:, None, :] * attn_sum).astype(
        jnp.bfloat16
    )
    resid_one = own_columns(resid_full, column_block, shard_width)
    mlp_in = modulate(resid_full, image_mod[:, 4], image_mod[:, 3])
    hidden_units = jax.nn.gelu(project(mlp_in, w_fc1), approximate=True).astype(jnp.bfloat16)
    mlp_sum = lax.psum_scatter(
        project(hidden_units, w_fc2).astype(jnp.bfloat16), "blk", scatter_dimension=2, tiled=True
    ).astype(jnp.float32)
    gate_mlp = own_columns(image_mod[:, 5], column_block, shard_width)
    resid_two = (resid_one.astype(jnp.float32) + gate_mlp[:, None, :] * mlp_sum).astype(
        jnp.bfloat16
    )
    stream = resid_two.astype(jnp.float32)
    row_sum, row_squares = lax.psum(
        (jnp.sum(stream, axis=-1), jnp.sum(stream * stream, axis=-1)), "blk"
    )
    center = row_sum / model_width
    spread = row_squares / model_width - center * center
    final_mod = out_mod[0]
    final_scale = own_columns(final_mod[:, 0], column_block, shard_width)
    final_shift = own_columns(final_mod[:, 1], column_block, shard_width)
    final_in = (
        (stream - center[..., None])
        * lax.rsqrt(spread[..., None] + EPSILON)
        * (1.0 + final_scale[:, None, :])
        + final_shift[:, None, :]
    ).astype(jnp.bfloat16)
    velocity_part = project(final_in, w_proj)
    half_index = lax.axis_index("cfg")
    channel_width = latent.shape[2]
    guide_scale = guide[:, None, None]
    velocity = lax.psum(velocity_part.astype(jnp.bfloat16), "blk").astype(jnp.float32)
    outgoing = own_columns(velocity, 1 - half_index, channel_width)
    other_half = from_partner(outgoing.astype(jnp.bfloat16), "cfg", 0).astype(outgoing.dtype)
    own_half = own_columns(velocity, half_index, channel_width)
    velocity_cond = jnp.where(half_index == 0, own_half, other_half)
    velocity_uncond = jnp.where(half_index == 0, other_half, own_half)
    guided = velocity_uncond + guide_scale * (velocity_cond - velocity_uncond)
    step_size = noise_level(t_index + stride) - noise_level(t_index)
    update = step_size[:, None, None] * guided
    new_latent = latent + update
    local_peak = jnp.max(jnp.abs(update), axis=(1, 2))
    peak_value = lax.pmax(local_peak, ("cfg", "seq"))
    return (new_latent, peak_value)


def solution(mesh):
    placed = (
        P("cfg", None, "seq", "blk"),
        P("cfg", None, "seq", "blk"),
        P("cfg", None, None, None),
        P("cfg", None, None, None),
        P("cfg", None, None, None),
        P(None, None, "blk"),
        P(None, None, "blk"),
        P("blk", None),
        P(None, "blk"),
        P("blk", None),
        P("blk", None),
        P(None, "seq", "cfg"),
        P("cfg", None),
        P(),
        P(),
        P(),
    )
    return jax.shard_map(
        per_device,
        mesh=mesh,
        in_specs=placed,
        out_specs=(P(None, "seq", "cfg"), P()),
        check_vma=False,
    )
```

profile of v0, /device:TPU:0, one launch (start us, length us, event | category | flops | bytes accessed | tf_op | source)
XLA Modules:
  0.0 552.0 jit_solution(2850391820597721948)
XLA Ops:
  9.6 46.8 %all-gather.10.cloned.1.call-done = bf16[1,2,512,1536]{3,2,1,0:T(8,128)(2,1)} async-done(((bf16[1,2,512,384]{3,2,1,0:T(8,128)(2,1)}), bf16[1,2,512,1536]{3,2,1,0:T(8,128)(2,1)}) %all-gather.10.cloned.1.call-update) | async-done | bytes 3145744 | tf_op jit(solution)/shard_map/all_gather | solution.py:68
  64.4 5.0 convolution_convert_fusion.3
  69.5 9.2 %all-gather.1 = bf16[1,2,40,1536]{3,2,1,0:T(8,128)(2,1)S(1)} all-gather(bf16[1,2,40,384]{3,2,1,0:T(8,128)(2,1)S(1)} %copy-done.12), channel_id=3, replica_groups=mesh['cfg'=2,'seq'=4,'blk'=4] {'blk'}, dimensions={3}, use_global_device_ids=true | all-gather | bytes 307200 | tf_op jit(solution)/shard_map/all_gather | solution.py:69
  80.8 16.4 %all_gather.22 = bf16[2,160,384]{2,1,0:T(8,128)(2,1)} all-gather(bf16[2,40,384]{2,1,0:T(8,128)(2,1)S(1)} %fusion.79), channel_id=1, replica_groups=mesh['cfg'=2,'seq'=4,'blk'=4] {'seq'}, dimensions={1}, use_global_device_ids=true | all-gather | bytes 307200 | tf_op jit(solution)/shard_map/all_gather | solution.py:128
  100.0 16.7 %all_gather.23 = bf16[2,160,384]{2,1,0:T(8,128)(2,1)S(1)} all-gather(bf16[2,40,384]{2,1,0:T(8,128)(2,1)S(1)} %fusion.82), channel_id=1, replica_groups=mesh['cfg'=2,'seq'=4,'blk'=4] {'seq'}, dimensions={1}, use_global_device_ids=true | all-gather | bytes 307200 | tf_op jit(solution)/shard_map/all_gather | solution.py:129
  125.9 9.6 %all-gather.8.cloned.1.call-done = bf16[2,2048,384]{2,1,0:T(8,128)(2,1)} async-done(((bf16[2,512,384]{2,1,0:T(8,128)(2,1)}), bf16[2,2048,384]{2,1,0:T(8,128)(2,1)}) %all-gather.8.cloned.1.call-update) | async-done | bytes 3145744 | tf_op jit(solution)/shard_map/all_gather | solution.py:116
  140.2 59.2 %all-gather.6.cloned.1.call-done = bf16[2,2048,384]{2,1,0:T(8,128)(2,1)} async-done(((bf16[2,512,384]{2,1,0:T(8,128)(2,1)}), bf16[2,2048,384]{2,1,0:T(8,128)(2,1)}) %all-gather.6.cloned.1.call-update) | async-done | bytes 3145744 | tf_op jit(solution)/shard_map/all_gather | solution.py:115
  199.4 4.7 copy.36
  204.1 87.5 %while.15 = (s32[]{:T(128)}, f32[2,6,512,64]{2,3,1,0:T(8,128)S(1)}, f32[2,6,512]{2,1,0:T(8,128)}, f32[2,6,512]{2,1,0:T(8,128)}, bf16[4,2,512,384]{2,3,1,0:T(8,12...) while((s32[]{:T(128)}, f32[2,6,512,64]{2,3,1,0:T(8,128)S(1)}, ...), condition=%wide.region_5.0_spmd.clone, body=%wide.region_2.5_spmd.clone.sunk | while | flops 831682560 | bytes 97419496 | solution.py:126
  205.5 8.1 %bitcast_reduce_fusion.2 = (f32[2,6,512]{2,1,0:T(8,128)}, f32[2,6,512,512]{3,2,1,0:T(8,128)}) fusion(bf16[2,512,6,64]{1,3,2,0:T(8,128)(2,1)S(1)} %bitcast.165, bf16[2,512,6,64]{1,3,2,0:T(8,128)(2,1)} %get-tuple-element.199), kind=kOutput, calls=%fused_computation.1.clone.1 | convolution fusion | flops 408938496 | bytes 14180352 | tf_op jit(solution)/shard_map/while/body/eval_jaxpr/pqhe,pkhe->phqk/dot_general | solution.py:91
  214.4 6.8 %fusion.134 = f32[2,6,512]{2,1,0:T(8,128)S(1)} fusion(f32[2,6,512,512]{3,2,1,0:T(8,128)} %get-tuple-element.172, f32[2,6,512]{2,1,0:T(8,128)S(1)} %select_maximum_fusion.2), kind=kLoop, calls=%fused_computation.3.clone.1 | loop fusion | flops 9431040 | bytes 12632064 | tf_op jit(solution)/shard_map/while/body/eval_jaxpr/reduce_sum | solution.py:99
  227.4 8.1 %bitcast_reduce_fusion.2 = (f32[2,6,512]{2,1,0:T(8,128)}, f32[2,6,512,512]{3,2,1,0:T(8,128)}) fusion(bf16[2,512,6,64]{1,3,2,0:T(8,128)(2,1)S(1)} %bitcast.165, bf16[2,512,6,64]{1,3,2,0:T(8,128)(2,1)} %get-tuple-element.199), kind=kOutput, calls=%fused_computation.1.clone.1 | convolution fusion | flops 408938496 | bytes 14180352 | tf_op jit(solution)/shard_map/while/body/eval_jaxpr/pqhe,pkhe->phqk/dot_general | solution.py:91
  236.3 6.8 %fusion.134 = f32[2,6,512]{2,1,0:T(8,128)S(1)} fusion(f32[2,6,512,512]{3,2,1,0:T(8,128)} %get-tuple-element.172, f32[2,6,512]{2,1,0:T(8,128)S(1)} %select_maximum_fusion.2), kind=kLoop, calls=%fused_computation.3.clone.1 | loop fusion | flops 9431040 | bytes 12632064 | tf_op jit(solution)/shard_map/while/body/eval_jaxpr/reduce_sum | solution.py:99
  249.3 8.1 %bitcast_reduce_fusion.2 = (f32[2,6,512]{2,1,0:T(8,128)}, f32[2,6,512,512]{3,2,1,0:T(8,128)}) fusion(bf16[2,512,6,64]{1,3,2,0:T(8,128)(2,1)S(1)} %bitcast.165, bf16[2,512,6,64]{1,3,2,0:T(8,128)(2,1)} %get-tuple-element.199), kind=kOutput, calls=%fused_computation.1.clone.1 | convolution fusion | flops 408938496 | bytes 14180352 | tf_op jit(solution)/shard_map/while/body/eval_jaxpr/pqhe,pkhe->phqk/dot_general | solution.py:91
  258.2 6.8 %fusion.134 = f32[2,6,512]{2,1,0:T(8,128)S(1)} fusion(f32[2,6,512,512]{3,2,1,0:T(8,128)} %get-tuple-element.172, f32[2,6,512]{2,1,0:T(8,128)S(1)} %select_maximum_fusion.2), kind=kLoop, calls=%fused_computation.3.clone.1 | loop fusion | flops 9431040 | bytes 12632064 | tf_op jit(solution)/shard_map/while/body/eval_jaxpr/reduce_sum | solution.py:99
  271.2 8.1 %bitcast_reduce_fusion.2 = (f32[2,6,512]{2,1,0:T(8,128)}, f32[2,6,512,512]{3,2,1,0:T(8,128)}) fusion(bf16[2,512,6,64]{1,3,2,0:T(8,128)(2,1)S(1)} %bitcast.165, bf16[2,512,6,64]{1,3,2,0:T(8,128)(2,1)} %get-tuple-element.199), kind=kOutput, calls=%fused_computation.1.clone.1 | convolution fusion | flops 408938496 | bytes 14180352 | tf_op jit(solution)/shard_map/while/body/eval_jaxpr/pqhe,pkhe->phqk/dot_general | solution.py:91
  280.1 6.8 %fusion.134 = f32[2,6,512]{2,1,0:T(8,128)S(1)} fusion(f32[2,6,512,512]{3,2,1,0:T(8,128)} %get-tuple-element.172, f32[2,6,512]{2,1,0:T(8,128)S(1)} %select_maximum_fusion.2), kind=kLoop, calls=%fused_computation.3.clone.1 | loop fusion | flops 9431040 | bytes 12632064 | tf_op jit(solution)/shard_map/while/body/eval_jaxpr/reduce_sum | solution.py:99
  301.8 85.9 %all-reduce.4.cloned.1.call-done = bf16[2,512,1536]{2,1,0:T(8,128)(2,1)} async-done(((bf16[2,512,1536]{2,1,0:T(8,128)(2,1)}), bf16[2,512,1536]{2,1,0:T(8,128)(2,1)}) %all-reduce.4.cloned.1.call-update) | async-done | bytes 3145744 | tf_op jit(solution)/shard_map/psum | solution.py:139
  394.4 15.8 %fusion.38 = bf16[2,512,1536]{2,1,0:T(8,128)(2,1)} fusion(bf16[1536,1536]{1,0:T(8,128)(2,1)} %param.27, bf16[1536,1536]{1,0:T(8,128)(2,1)} %param.26, bf16[2,512,1536]{2,1,0:T(8,128)(2,1)} %copy-done.4, f32[2,1536]{1,0:T(2,128)S(1)} %get-tuple-element.113, f32[2,1536]{1,0:T(2,128)S(1)} %get-tuple-element.114, f32[2,512]{1,0:T(2,128)S(1)} %add_rsqrt_fusion.1, ...), kind=kOutput, calls=%fused_computation.50 | convolution fusion | flops 9688842240 | bytes 15761408 | tf_op jit(solution)/shard_map/dot_general | solution.py:31
  410.2 8.7 %copy.44 = bf16[2,512,1536]{1,0,2:T(2,128)(2,1)} copy(bf16[2,512,1536]{2,1,0:T(8,128)(2,1)} %fusion.38) | data formatting | bytes 6291456
  424.2 43.3 %reduce-scatter.4.cloned.1.call-done = bf16[384,1024]{1,0:T(8,128)(2,1)} async-done(((bf16[1536,1024]{1,0:T(8,128)(2,1)}), bf16[384,1024]{1,0:T(8,128)(2,1)}) %reduce-scatter.4.cloned.1.call-update) | async-done | bytes 786448
  472.4 9.1 %all-reduce = (f32[2,512]{1,0:T(2,128)S(1)}, f32[2,512]{1,0:T(2,128)S(1)}) all-reduce(f32[2,512]{1,0:T(2,128)S(1)} %get-tuple-element.69, f32[2,512]{1,0:T(2,128)S(1)} %get-tuple-element.68), channel_id=1, replica_groups=mesh['cfg'=2,'seq'=4,'blk'=4] {'blk'}, use_global_device_ids=true, to_apply=%region_17.18 | all-reduce | flops 2048 | bytes 16384 | tf_op jit(solution)/shard_map/psum | solution.py:154
  482.7 42.1 %all-reduce.6.cloned.1.call-done = bf16[2,512,64]{1,2,0:T(8,128)(2,1)} async-done(((bf16[2,512,64]{1,2,0:T(8,128)(2,1)}), bf16[2,512,64]{1,2,0:T(8,128)(2,1)}) %all-reduce.6.cloned.1.call-update) | async-done | bytes 131088 | tf_op jit(solution)/shard_map/psum | solution.py:172
  527.9 17.2 %pmax.7 = f32[2]{0:T(128)} all-reduce(f32[2]{0:T(128)S(1)} %get-tuple-element.97), channel_id=1, replica_groups=mesh['cfg'=2,'seq'=4,'blk'=4] {'cfg','seq'}, use_global_device_ids=true, to_apply=%region_20.21 | all-reduce | flops 2 | bytes 16 | tf_op jit(solution)/shard_map/pmax | solution.py:183
  (154 shorter events, 87.8 us)
Async XLA Ops:
  7.2 291.0 %copy-start = (bf16[384,1536]{1,0:T(8,128)(2,1)S(1)}, bf16[384,1536]{1,0:T(8,128)(2,1)}, u32[]{:S(2)}) copy-start(bf16[384,1536]{1,0:T(8,128)(2,1)} %param.25) | copy-start | bytes 3538948
  7.2 49.2 %all-gather.10.cloned.1.call-start = ((), (), s32[]{:S(2)}) async-start(), calls=%async_computation.5 | async-start | bytes 3932160 | tf_op jit(solution)/shard_map/all_gather | solution.py:68
  7.9 127.6 %all-gather.8.cloned.1.call-start = ((), (), s32[]{:S(2)}) async-start(), calls=%async_computation.2 | async-start | bytes 3932160 | tf_op jit(solution)/shard_map/all_gather | solution.py:116
  64.3 14.7 %copy-start.15 = (f32[1,2,2,1536]{3,2,1,0:T(2,128)S(1)}, f32[1,2,2,1536]{3,2,1,0:T(2,128)}, u32[]{:S(2)}) copy-start(f32[1,2,2,1536]{3,2,1,0:T(2,128)} %param.21) | copy-start | bytes 73732
  64.3 135.0 %all-gather.6.cloned.1.call-start = ((), (), s32[]{:S(2)}) async-start(), calls=%async_computation.1 | async-start | bytes 3932160 | tf_op jit(solution)/shard_map/all_gather | solution.py:115
  69.3 48.2 %copy-start.19 = (s32[1,2]{1,0:T(1,128)S(1)}, s32[1,2]{1,0:T(1,128)}, u32[]{:S(2)}) copy-start(s32[1,2]{1,0:T(1,128)} %param.30) | copy-start | bytes 28
  69.4 318.3 %all-reduce.4.cloned.1.call-start = ((), (), s32[]{:S(2)}) async-start(), calls=%async_computation.3 | async-start | bytes 6291456 | tf_op jit(solution)/shard_map/psum | solution.py:139
  214.4 6.9 %copy-start.6 = (f32[2,6,512]{2,1,0:T(8,128)S(1)}, f32[2,6,512]{2,1,0:T(8,128)}, u32[]{:S(2)}) copy-start(f32[2,6,512]{2,1,0:T(8,128)} %get-tuple-element.187) | copy-start | bytes 73732 | tf_op jit(solution)/shard_map/while
  214.4 6.9 %copy-start.8 = (f32[2,6,512]{2,1,0:T(8,128)S(1)}, f32[2,6,512]{2,1,0:T(8,128)}, u32[]{:S(2)}) copy-start(f32[2,6,512]{2,1,0:T(8,128)} %get-tuple-element.188) | copy-start | bytes 73732 | tf_op jit(solution)/shard_map/while
  214.4 8.2 %copy-start.1 = (f32[2,6,512,512]{3,2,1,0:T(8,128)S(1)}, f32[2,6,512,512]{3,2,1,0:T(8,128)}, u32[]{:S(2)}) copy-start(f32[2,6,512,512]{3,2,1,0:T(8,128)} %get-tuple-element.172) | copy-start | bytes 37748740 | tf_op jit(solution)/shard_map/while
  236.3 6.9 %copy-start.8 = (f32[2,6,512]{2,1,0:T(8,128)S(1)}, f32[2,6,512]{2,1,0:T(8,128)}, u32[]{:S(2)}) copy-start(f32[2,6,512]{2,1,0:T(8,128)} %get-tuple-element.188) | copy-start | bytes 73732 | tf_op jit(solution)/shard_map/while
  236.3 8.2 %copy-start.1 = (f32[2,6,512,512]{3,2,1,0:T(8,128)S(1)}, f32[2,6,512,512]{3,2,1,0:T(8,128)}, u32[]{:S(2)}) copy-start(f32[2,6,512,512]{3,2,1,0:T(8,128)} %get-tuple-element.172) | copy-start | bytes 37748740 | tf_op jit(solution)/shard_map/while
  258.2 6.9 %copy-start.8 = (f32[2,6,512]{2,1,0:T(8,128)S(1)}, f32[2,6,512]{2,1,0:T(8,128)}, u32[]{:S(2)}) copy-start(f32[2,6,512]{2,1,0:T(8,128)} %get-tuple-element.188) | copy-start | bytes 73732 | tf_op jit(solution)/shard_map/while
  258.2 8.2 %copy-start.1 = (f32[2,6,512,512]{3,2,1,0:T(8,128)S(1)}, f32[2,6,512,512]{3,2,1,0:T(8,128)}, u32[]{:S(2)}) copy-start(f32[2,6,512,512]{3,2,1,0:T(8,128)} %get-tuple-element.172) | copy-start | bytes 37748740 | tf_op jit(solution)/shard_map/while
  280.1 6.9 %copy-start.8 = (f32[2,6,512]{2,1,0:T(8,128)S(1)}, f32[2,6,512]{2,1,0:T(8,128)}, u32[]{:S(2)}) copy-start(f32[2,6,512]{2,1,0:T(8,128)} %get-tuple-element.188) | copy-start | bytes 73732 | tf_op jit(solution)/shard_map/while
  280.1 8.2 %copy-start.1 = (f32[2,6,512,512]{3,2,1,0:T(8,128)S(1)}, f32[2,6,512,512]{3,2,1,0:T(8,128)}, u32[]{:S(2)}) copy-start(f32[2,6,512,512]{3,2,1,0:T(8,128)} %get-tuple-element.172) | copy-start | bytes 37748740 | tf_op jit(solution)/shard_map/while
  301.7 165.8 %reduce-scatter.4.cloned.1.call-start = ((), (), s32[]{:S(2)}) async-start(), calls=%async_computation.6 | async-start | bytes 3932160
  423.3 58.2 %copy-start.18 = (bf16[384,64]{0,1:T(8,128)(2,1)S(1)}, bf16[384,64]{0,1:T(8,128)(2,1)}, u32[]{:S(2)}) copy-start(bf16[384,64]{0,1:T(8,128)(2,1)} %param.28) | copy-start | bytes 147460
  423.3 101.5 %all-reduce.6.cloned.1.call-start = ((), (), s32[]{:S(2)}) async-start(), calls=%async_computation.4 | async-start | bytes 262144 | tf_op jit(solution)/shard_map/psum | solution.py:172
  424.1 101.7 %copy-start.20 = (s32[2]{0:T(128)S(1)}, s32[2]{0:T(128)}, u32[]{:S(2)}) copy-start(s32[2]{0:T(128)} %param.31) | copy-start | bytes 28
  424.2 101.7 %copy-start.21 = (s32[2]{0:T(128)S(1)}, s32[2]{0:T(128)}, u32[]{:S(2)}) copy-start(s32[2]{0:T(128)} %param.32) | copy-start | bytes 28
  424.2 103.0 %copy-start.11 = (f32[2,512,32]{1,2,0:T(8,128)S(1)}, f32[2,512,32]{1,2,0:T(8,128)}, u32[]{:S(2)}) copy-start(f32[2,512,32]{1,2,0:T(8,128)} %param.29) | copy-start | bytes 393220
  424.2 102.9 %copy-start.17 = (f32[2]{0:T(128)S(1)}, f32[2]{0:T(128)}, u32[]{:S(2)}) copy-start(f32[2]{0:T(128)} %param.33) | copy-start | bytes 28
  525.8 1.3 collective-permute-start
  (17 other events, 72.4 us)
Sparse Core Ops, SparseCore 0:
  9.8 46.5 all-gather.9
  64.4 71.0 all-gather.7
  137.1 62.2 all-gather.5
  301.8 85.8 all-reduce.3
  423.4 43.9 reduce-scatter.3
  482.9 41.9 all-reduce.5
where the time goes:
time: 553 us; the launch traced here: 552 us
  waiting for transfers between devices  289 us (52%)
  matrix products  85.7 us (15%)
  blocking collectives  68.6 us (12%)
  other arithmetic  47.8 us (9%)
  local copies, waits for them, and re-layouts  45.9 us (8%)
  between operations  14.5 us (3%)
    psum x1, waiting for transfers between devices, per_device(): lax.psum(attn_part.astype(jnp.bfloat16), 'blk').astype(jnp.float32)  85.9 us
    all_gather x1, waiting for transfers between devices, per_device(): key_piece = lax.all_gather(keys_img, 'seq', axis=1, tiled=True)  59.2 us
    all_gather x1, waiting for transfers between devices, per_device(): lax.all_gather(img_hidden[0], 'blk', axis=2, tiled=True)  46.8 us
    unnamed x7, waiting for transfers between devices  44 us
    psum x1, waiting for transfers between devices, per_device(): lax.psum(velocity_part.astype(jnp.bfloat16), 'blk').astype(jnp.float32)  42.1 us
    dot_general x8, matrix products, project(): result = jnp.dot(flat_rows, weight, preferred_element_type=jnp.float32)  37 us
    dot_general x5, matrix products, attend_block(): jnp.einsum('pqhe,pkhe->phqk', query_heads, key_heads, preferred_element_t...  35.9 us
    reduce_sum x5, other arithmetic, attend_block(): denominator = denominator * factor + jnp.sum(weights, axis=-1)  30.6 us
  transfers between devices with their start and end apart: 7, of which 7 were waited for; matrix products, arithmetic and copies ran while one was open for 5% of the time, Pallas kernels for 0%

commit v1 on v0

--- a/solution.py
+++ b/solution.py
@@ -136,7 +136,9 @@
     attended = (accumulated / denominator[..., None]).astype(jnp.bfloat16)
     attended = attended.transpose(0, 2, 1, 3).reshape(prompts, img_rows, head_width)
     attn_part = project(attended, w_out)
-    attn_sum = lax.psum(attn_part.astype(jnp.bfloat16), "blk").astype(jnp.float32)
+    attn_sum = jnp.sum(lax.all_gather(attn_part.astype(jnp.bfloat16), "blk"), axis=0).astype(
+        jnp.float32
+    )
     resid_full = (image_full.astype(jnp.float32) + image_mod[:, 2][:, None, :] * attn_sum).astype(
         jnp.bfloat16
     )

time: 553 us -> 598 us (1.081)
  waiting for transfers between devices: 289 us -> 324 us
  other arithmetic: 47.8 us -> 56.9 us
    all_gather x0 -> x1, waiting for transfers between devices: none -> 121 us  [per_device(): lax.all_gather(attn_part.astype(jnp.bfloat16), 'blk')]
    psum x1 -> x0, waiting for transfers between devices: 85.9 us -> none  [per_device(): lax.psum(attn_part.astype(jnp.bfloat16), 'blk').astype(jnp.float32)]
    reduce_sum x0 -> x1, other arithmetic: none -> 9.08 us  [per_device(): jnp.sum(lax.all_gather(attn_part.astype(jnp.bfloat16), 'blk'), axis=0)]
  transfers between devices with their start and end apart: 7 -> 7, of which waited for: 7 -> 7; matrix products, arithmetic and copies ran while one was open for 5% -> 4% of each run, Pallas kernels for 0% -> 0%
where the time goes in v1:
time: 598 us; the launch traced here: 596 us
  waiting for transfers between devices  324 us (54%)
  matrix products  85.4 us (14%)
  blocking collectives  68.5 us (11%)
  other arithmetic  56.9 us (10%)
  local copies, waits for them, and re-layouts  45.9 us (8%)
  between operations  14.5 us (2%)
    all_gather x1, waiting for transfers between devices, per_device(): lax.all_gather(attn_part.astype(jnp.bfloat16), 'blk')  121 us
    all_gather x1, waiting for transfers between devices, per_device(): key_piece = lax.all_gather(keys_img, 'seq', axis=1, tiled=True)  59.2 us
    all_gather x1, waiting for transfers between devices, per_device(): lax.all_gather(img_hidden[0], 'blk', axis=2, tiled=True)  46.8 us
    unnamed x7, waiting for transfers between devices  43.8 us
    psum x1, waiting for transfers between devices, per_device(): lax.psum(velocity_part.astype(jnp.bfloat16), 'blk').astype(jnp.float32)  42.1 us
    dot_general x8, matrix products, project(): result = jnp.dot(flat_rows, weight, preferred_element_type=jnp.float32)  36.7 us
    dot_general x5, matrix products, attend_block(): jnp.einsum('pqhe,pkhe->phqk', query_heads, key_heads, preferred_element_t...  35.9 us
    reduce_sum x5, other arithmetic, attend_block(): denominator = denominator * factor + jnp.sum(weights, axis=-1)  30.6 us
  transfers between devices with their start and end apart: 7, of which 7 were waited for; matrix products, arithmetic and copies ran while one was open for 4% of the time, Pallas kernels for 0%

profile of v1, /device:TPU:0, one launch (start us, length us, event | category | flops | bytes accessed | tf_op | source)
XLA Modules:
  0.0 596.1 jit_solution(17292837516544759877)
XLA Ops:
  9.6 46.8 %all-gather.12.cloned.1.call-done = bf16[1,2,512,1536]{3,2,1,0:T(8,128)(2,1)} async-done(((bf16[1,2,512,384]{3,2,1,0:T(8,128)(2,1)}), bf16[1,2,512,1536]{3,2,1,0:T(8,128)(2,1)}) %all-gather.12.cloned.1.call-update) | async-done | bytes 3145744 | tf_op jit(solution)/shard_map/all_gather | solution.py:68
  64.4 5.0 convolution_convert_fusion.3
  69.5 9.2 %all-gather.1 = bf16[1,2,40,1536]{3,2,1,0:T(8,128)(2,1)S(1)} all-gather(bf16[1,2,40,384]{3,2,1,0:T(8,128)(2,1)S(1)} %copy-done.12), channel_id=3, replica_groups=mesh['cfg'=2,'seq'=4,'blk'=4] {'blk'}, dimensions={3}, use_global_device_ids=true | all-gather | bytes 307200 | tf_op jit(solution)/shard_map/all_gather | solution.py:69
  80.8 16.4 %all_gather.28 = bf16[2,160,384]{2,1,0:T(8,128)(2,1)} all-gather(bf16[2,40,384]{2,1,0:T(8,128)(2,1)S(1)} %fusion.79), channel_id=1, replica_groups=mesh['cfg'=2,'seq'=4,'blk'=4] {'seq'}, dimensions={1}, use_global_device_ids=true | all-gather | bytes 307200 | tf_op jit(solution)/shard_map/all_gather | solution.py:128
  100.0 16.6 %all_gather.29 = bf16[2,160,384]{2,1,0:T(8,128)(2,1)S(1)} all-gather(bf16[2,40,384]{2,1,0:T(8,128)(2,1)S(1)} %fusion.82), channel_id=1, replica_groups=mesh['cfg'=2,'seq'=4,'blk'=4] {'seq'}, dimensions={1}, use_global_device_ids=true | all-gather | bytes 307200 | tf_op jit(solution)/shard_map/all_gather | solution.py:129
  125.9 9.6 %all-gather.10.cloned.1.call-done = bf16[2,2048,384]{2,1,0:T(8,128)(2,1)} async-done(((bf16[2,512,384]{2,1,0:T(8,128)(2,1)}), bf16[2,2048,384]{2,1,0:T(8,128)(2,1)}) %all-gather.10.cloned.1.call-update) | async-done | bytes 3145744 | tf_op jit(solution)/shard_map/all_gather | solution.py:116
  140.2 59.2 %all-gather.8.cloned.1.call-done = bf16[2,2048,384]{2,1,0:T(8,128)(2,1)} async-done(((bf16[2,512,384]{2,1,0:T(8,128)(2,1)}), bf16[2,2048,384]{2,1,0:T(8,128)(2,1)}) %all-gather.8.cloned.1.call-update) | async-done | bytes 3145744 | tf_op jit(solution)/shard_map/all_gather | solution.py:115
  204.1 87.5 %while.15 = (s32[]{:T(128)}, f32[2,6,512,64]{2,3,1,0:T(8,128)S(1)}, f32[2,6,512]{2,1,0:T(8,128)}, f32[2,6,512]{2,1,0:T(8,128)}, bf16[4,2,512,384]{2,3,1,0:T(8,12...) while((s32[]{:T(128)}, f32[2,6,512,64]{2,3,1,0:T(8,128)S(1)}, ...), condition=%wide.region_5.0_spmd.clone, body=%wide.region_2.5_spmd.clone.sunk | while | flops 831682560 | bytes 97419496 | solution.py:126
  205.5 8.1 %bitcast_reduce_fusion.2 = (f32[2,6,512]{2,1,0:T(8,128)}, f32[2,6,512,512]{3,2,1,0:T(8,128)}) fusion(bf16[2,512,6,64]{1,3,2,0:T(8,128)(2,1)S(1)} %bitcast.166, bf16[2,512,6,64]{1,3,2,0:T(8,128)(2,1)} %get-tuple-element.199), kind=kOutput, calls=%fused_computation.1.clone.1 | convolution fusion | flops 408938496 | bytes 14180352 | tf_op jit(solution)/shard_map/while/body/eval_jaxpr/pqhe,pkhe->phqk/dot_general | solution.py:91
  214.4 6.8 %fusion.134 = f32[2,6,512]{2,1,0:T(8,128)S(1)} fusion(f32[2,6,512,512]{3,2,1,0:T(8,128)} %get-tuple-element.172, f32[2,6,512]{2,1,0:T(8,128)S(1)} %select_maximum_fusion.2), kind=kLoop, calls=%fused_computation.3.clone.1 | loop fusion | flops 9431040 | bytes 12632064 | tf_op jit(solution)/shard_map/while/body/eval_jaxpr/reduce_sum | solution.py:99
  227.4 8.1 %bitcast_reduce_fusion.2 = (f32[2,6,512]{2,1,0:T(8,128)}, f32[2,6,512,512]{3,2,1,0:T(8,128)}) fusion(bf16[2,512,6,64]{1,3,2,0:T(8,128)(2,1)S(1)} %bitcast.166, bf16[2,512,6,64]{1,3,2,0:T(8,128)(2,1)} %get-tuple-element.199), kind=kOutput, calls=%fused_computation.1.clone.1 | convolution fusion | flops 408938496 | bytes 14180352 | tf_op jit(solution)/shard_map/while/body/eval_jaxpr/pqhe,pkhe->phqk/dot_general | solution.py:91
  236.3 6.8 %fusion.134 = f32[2,6,512]{2,1,0:T(8,128)S(1)} fusion(f32[2,6,512,512]{3,2,1,0:T(8,128)} %get-tuple-element.172, f32[2,6,512]{2,1,0:T(8,128)S(1)} %select_maximum_fusion.2), kind=kLoop, calls=%fused_computation.3.clone.1 | loop fusion | flops 9431040 | bytes 12632064 | tf_op jit(solution)/shard_map/while/body/eval_jaxpr/reduce_sum | solution.py:99
  249.3 8.1 %bitcast_reduce_fusion.2 = (f32[2,6,512]{2,1,0:T(8,128)}, f32[2,6,512,512]{3,2,1,0:T(8,128)}) fusion(bf16[2,512,6,64]{1,3,2,0:T(8,128)(2,1)S(1)} %bitcast.166, bf16[2,512,6,64]{1,3,2,0:T(8,128)(2,1)} %get-tuple-element.199), kind=kOutput, calls=%fused_computation.1.clone.1 | convolution fusion | flops 408938496 | bytes 14180352 | tf_op jit(solution)/shard_map/while/body/eval_jaxpr/pqhe,pkhe->phqk/dot_general | solution.py:91
  258.2 6.8 %fusion.134 = f32[2,6,512]{2,1,0:T(8,128)S(1)} fusion(f32[2,6,512,512]{3,2,1,0:T(8,128)} %get-tuple-element.172, f32[2,6,512]{2,1,0:T(8,128)S(1)} %select_maximum_fusion.2), kind=kLoop, calls=%fused_computation.3.clone.1 | loop fusion | flops 9431040 | bytes 12632064 | tf_op jit(solution)/shard_map/while/body/eval_jaxpr/reduce_sum | solution.py:99
  271.2 8.1 %bitcast_reduce_fusion.2 = (f32[2,6,512]{2,1,0:T(8,128)}, f32[2,6,512,512]{3,2,1,0:T(8,128)}) fusion(bf16[2,512,6,64]{1,3,2,0:T(8,128)(2,1)S(1)} %bitcast.166, bf16[2,512,6,64]{1,3,2,0:T(8,128)(2,1)} %get-tuple-element.199), kind=kOutput, calls=%fused_computation.1.clone.1 | convolution fusion | flops 408938496 | bytes 14180352 | tf_op jit(solution)/shard_map/while/body/eval_jaxpr/pqhe,pkhe->phqk/dot_general | solution.py:91
  280.1 6.8 %fusion.134 = f32[2,6,512]{2,1,0:T(8,128)S(1)} fusion(f32[2,6,512,512]{3,2,1,0:T(8,128)} %get-tuple-element.172, f32[2,6,512]{2,1,0:T(8,128)S(1)} %select_maximum_fusion.2), kind=kLoop, calls=%fused_computation.3.clone.1 | loop fusion | flops 9431040 | bytes 12632064 | tf_op jit(solution)/shard_map/while/body/eval_jaxpr/reduce_sum | solution.py:99
  302.0 121.0 %all-gather.14.cloned.1.call-done = bf16[8,512,1536]{2,1,0:T(8,128)(2,1)} async-done(((bf16[2,512,1536]{2,1,0:T(8,128)(2,1)}), bf16[8,512,1536]{2,1,0:T(8,128)(2,1)}) %all-gather.14.cloned.1.call-update) | async-done | bytes 12582928 | tf_op jit(solution)/shard_map/all_gather | solution.py:139
  423.0 9.1 %reduce_sum.107 = bf16[2,512,1536]{2,1,0:T(8,128)(2,1)} reduce(bf16[4,2,512,1536]{3,2,1,0:T(8,128)(2,1)} %bitcast.171, bf16[]{:T(256)} %constant.75.clone.1), dimensions={0}, to_apply=%region_10.11 | reduce | flops 4718592 | bytes 15728642 | tf_op jit(solution)/shard_map/reduce_sum | solution.py:139
  438.7 15.6 %fusion.38 = bf16[2,512,1536]{2,1,0:T(8,128)(2,1)} fusion(bf16[1536,1536]{1,0:T(8,128)(2,1)} %param.27, bf16[1536,1536]{1,0:T(8,128)(2,1)} %param.26, bf16[2,512,1536]{2,1,0:T(8,128)(2,1)} %copy-done.4, f32[2,1536]{1,0:T(2,128)S(1)} %get-tuple-element.113, f32[2,1536]{1,0:T(2,128)S(1)} %get-tuple-element.114, f32[2,512]{1,0:T(2,128)S(1)} %add_rsqrt_fusion.1, ...), kind=kOutput, calls=%fused_computation.50 | convolution fusion | flops 9688842240 | bytes 15761408 | tf_op jit(solution)/shard_map/dot_general | solution.py:31
  454.4 8.7 %copy.44 = bf16[2,512,1536]{1,0,2:T(2,128)(2,1)} copy(bf16[2,512,1536]{2,1,0:T(8,128)(2,1)} %fusion.38) | data formatting | bytes 6291456
  468.6 43.0 %reduce-scatter.4.cloned.1.call-done = bf16[384,1024]{1,0:T(8,128)(2,1)} async-done(((bf16[1536,1024]{1,0:T(8,128)(2,1)}), bf16[384,1024]{1,0:T(8,128)(2,1)}) %reduce-scatter.4.cloned.1.call-update) | async-done | bytes 786448
  516.5 9.1 %all-reduce = (f32[2,512]{1,0:T(2,128)S(1)}, f32[2,512]{1,0:T(2,128)S(1)}) all-reduce(f32[2,512]{1,0:T(2,128)S(1)} %get-tuple-element.69, f32[2,512]{1,0:T(2,128)S(1)} %get-tuple-element.68), channel_id=1, replica_groups=mesh['cfg'=2,'seq'=4,'blk'=4] {'blk'}, use_global_device_ids=true, to_apply=%region_17.18 | all-reduce | flops 2048 | bytes 16384 | tf_op jit(solution)/shard_map/psum | solution.py:156
  526.9 42.1 %all-reduce.3.cloned.1.call-done = bf16[2,512,64]{1,2,0:T(8,128)(2,1)} async-done(((bf16[2,512,64]{1,2,0:T(8,128)(2,1)}), bf16[2,512,64]{1,2,0:T(8,128)(2,1)}) %all-reduce.3.cloned.1.call-update) | async-done | bytes 131088 | tf_op jit(solution)/shard_map/psum | solution.py:174
  572.0 17.2 %pmax.7 = f32[2]{0:T(128)} all-reduce(f32[2]{0:T(128)S(1)} %get-tuple-element.97), channel_id=1, replica_groups=mesh['cfg'=2,'seq'=4,'blk'=4] {'cfg','seq'}, use_global_device_ids=true, to_apply=%region_20.21 | all-reduce | flops 2 | bytes 16 | tf_op jit(solution)/shard_map/pmax | solution.py:185
  (155 shorter events, 92.9 us)
Async XLA Ops:
  7.2 291.0 %copy-start = (bf16[384,1536]{1,0:T(8,128)(2,1)S(1)}, bf16[384,1536]{1,0:T(8,128)(2,1)}, u32[]{:S(2)}) copy-start(bf16[384,1536]{1,0:T(8,128)(2,1)} %param.25) | copy-start | bytes 3538948
  7.2 49.2 %all-gather.12.cloned.1.call-start = ((), (), s32[]{:S(2)}) async-start(), calls=%async_computation.4 | async-start | bytes 3932160 | tf_op jit(solution)/shard_map/all_gather | solution.py:68
  7.9 127.6 %all-gather.10.cloned.1.call-start = ((), (), s32[]{:S(2)}) async-start(), calls=%async_computation.2 | async-start | bytes 3932160 | tf_op jit(solution)/shard_map/all_gather | solution.py:116
  64.3 14.7 %copy-start.15 = (f32[1,2,2,1536]{3,2,1,0:T(2,128)S(1)}, f32[1,2,2,1536]{3,2,1,0:T(2,128)}, u32[]{:S(2)}) copy-start(f32[1,2,2,1536]{3,2,1,0:T(2,128)} %param.21) | copy-start | bytes 73732
  64.3 135.0 %all-gather.8.cloned.1.call-start = ((), (), s32[]{:S(2)}) async-start(), calls=%async_computation.1 | async-start | bytes 3932160 | tf_op jit(solution)/shard_map/all_gather | solution.py:115
  69.3 48.2 %copy-start.19 = (s32[1,2]{1,0:T(1,128)S(1)}, s32[1,2]{1,0:T(1,128)}, u32[]{:S(2)}) copy-start(s32[1,2]{1,0:T(1,128)} %param.30) | copy-start | bytes 28
  69.4 353.6 %all-gather.14.cloned.1.call-start = ((), (), s32[]{:S(2)}) async-start(), calls=%async_computation.5 | async-start | bytes 15728640 | tf_op jit(solution)/shard_map/all_gather | solution.py:139
  214.4 6.9 %copy-start.6 = (f32[2,6,512]{2,1,0:T(8,128)S(1)}, f32[2,6,512]{2,1,0:T(8,128)}, u32[]{:S(2)}) copy-start(f32[2,6,512]{2,1,0:T(8,128)} %get-tuple-element.187) | copy-start | bytes 73732 | tf_op jit(solution)/shard_map/while
  214.4 6.9 %copy-start.8 = (f32[2,6,512]{2,1,0:T(8,128)S(1)}, f32[2,6,512]{2,1,0:T(8,128)}, u32[]{:S(2)}) copy-start(f32[2,6,512]{2,1,0:T(8,128)} %get-tuple-element.188) | copy-start | bytes 73732 | tf_op jit(solution)/shard_map/while
  214.4 8.2 %copy-start.1 = (f32[2,6,512,512]{3,2,1,0:T(8,128)S(1)}, f32[2,6,512,512]{3,2,1,0:T(8,128)}, u32[]{:S(2)}) copy-start(f32[2,6,512,512]{3,2,1,0:T(8,128)} %get-tuple-element.172) | copy-start | bytes 37748740 | tf_op jit(solution)/shard_map/while
  236.3 6.9 %copy-start.8 = (f32[2,6,512]{2,1,0:T(8,128)S(1)}, f32[2,6,512]{2,1,0:T(8,128)}, u32[]{:S(2)}) copy-start(f32[2,6,512]{2,1,0:T(8,128)} %get-tuple-element.188) | copy-start | bytes 73732 | tf_op jit(solution)/shard_map/while
  236.3 8.2 %copy-start.1 = (f32[2,6,512,512]{3,2,1,0:T(8,128)S(1)}, f32[2,6,512,512]{3,2,1,0:T(8,128)}, u32[]{:S(2)}) copy-start(f32[2,6,512,512]{3,2,1,0:T(8,128)} %get-tuple-element.172) | copy-start | bytes 37748740 | tf_op jit(solution)/shard_map/while
  258.2 6.9 %copy-start.8 = (f32[2,6,512]{2,1,0:T(8,128)S(1)}, f32[2,6,512]{2,1,0:T(8,128)}, u32[]{:S(2)}) copy-start(f32[2,6,512]{2,1,0:T(8,128)} %get-tuple-element.188) | copy-start | bytes 73732 | tf_op jit(solution)/shard_map/while
  258.2 8.2 %copy-start.1 = (f32[2,6,512,512]{3,2,1,0:T(8,128)S(1)}, f32[2,6,512,512]{3,2,1,0:T(8,128)}, u32[]{:S(2)}) copy-start(f32[2,6,512,512]{3,2,1,0:T(8,128)} %get-tuple-element.172) | copy-start | bytes 37748740 | tf_op jit(solution)/shard_map/while
  280.1 6.9 %copy-start.8 = (f32[2,6,512]{2,1,0:T(8,128)S(1)}, f32[2,6,512]{2,1,0:T(8,128)}, u32[]{:S(2)}) copy-start(f32[2,6,512]{2,1,0:T(8,128)} %get-tuple-element.188) | copy-start | bytes 73732 | tf_op jit(solution)/shard_map/while
  280.1 8.2 %copy-start.1 = (f32[2,6,512,512]{3,2,1,0:T(8,128)S(1)}, f32[2,6,512,512]{3,2,1,0:T(8,128)}, u32[]{:S(2)}) copy-start(f32[2,6,512,512]{3,2,1,0:T(8,128)} %get-tuple-element.172) | copy-start | bytes 37748740 | tf_op jit(solution)/shard_map/while
  301.6 210.0 %reduce-scatter.4.cloned.1.call-start = ((), (), s32[]{:S(2)}) async-start(), calls=%async_computation.6 | async-start | bytes 3932160
  467.4 58.2 %copy-start.18 = (bf16[384,64]{0,1:T(8,128)(2,1)S(1)}, bf16[384,64]{0,1:T(8,128)(2,1)}, u32[]{:S(2)}) copy-start(bf16[384,64]{0,1:T(8,128)(2,1)} %param.28) | copy-start | bytes 147460
  467.5 101.5 %all-reduce.3.cloned.1.call-start = ((), (), s32[]{:S(2)}) async-start(), calls=%async_computation.3 | async-start | bytes 262144 | tf_op jit(solution)/shard_map/psum | solution.py:174
  468.6 101.5 %copy-start.20 = (s32[2]{0:T(128)S(1)}, s32[2]{0:T(128)}, u32[]{:S(2)}) copy-start(s32[2]{0:T(128)} %param.31) | copy-start | bytes 28
  468.6 101.5 %copy-start.21 = (s32[2]{0:T(128)S(1)}, s32[2]{0:T(128)}, u32[]{:S(2)}) copy-start(s32[2]{0:T(128)} %param.32) | copy-start | bytes 28
  468.6 102.7 %copy-start.11 = (f32[2,512,32]{1,2,0:T(8,128)S(1)}, f32[2,512,32]{1,2,0:T(8,128)}, u32[]{:S(2)}) copy-start(f32[2,512,32]{1,2,0:T(8,128)} %param.29) | copy-start | bytes 393220
  468.6 102.7 %copy-start.17 = (f32[2]{0:T(128)S(1)}, f32[2]{0:T(128)}, u32[]{:S(2)}) copy-start(f32[2]{0:T(128)} %param.33) | copy-start | bytes 28
  569.9 1.3 collective-permute-start
  (17 other events, 73.0 us)
Sparse Core Ops, SparseCore 0:
  9.8 46.5 all-gather.11
  64.4 71.0 all-gather.9
  137.1 62.2 all-gather.7
  301.8 121.1 all-gather.13
  467.6 43.9 reduce-scatter.3
  527.0 41.9 all-reduce.2
